TPU v7x, 32 devices: a whole 2x2x4 slice. The times are simulated.
32 devices in a mesh: rep: 16 (over z, x, core), fsdp: 2 (over y).
Axes of the slice: x: 2, y: 2, z: 4, core: 2. Of those that a mesh axis runs over, the one named last changes fastest.
Arguments:
- activations: bfloat16 [8192, 4096], P(('rep', 'fsdp')), may hold values from -6 to 6
- cotangent: bfloat16 [8192, 512], P(('rep', 'fsdp')), may hold values from -0.25 to 0.25
- momentum: bfloat16 [16, 4096, 512], P('rep', 'fsdp'), may hold values from -6 to 6
Outputs:
- new_momentum: bfloat16 [16, 4096, 512], P('rep', 'fsdp')
- update: bfloat16 [4096, 512], P('fsdp')
All inputs are finite; a program needn't handle non-finite values.
Results may differ from a plain program's by a relative error of at most 0.001.
Values may be sent and summed in bfloat16 or wider, within the bound.
A program may use at most 64 MiB of HBM per device.

v0:
```python
import math

import jax
import jax.numpy as jnp
from jax import lax
from jax.sharding import PartitionSpec as P

BLOCK = 64
KEEP = 16


def dct_basis():
    freq = jnp.arange(KEEP, dtype=jnp.float32)[:, None]
    place = jnp.arange(BLOCK, dtype=jnp.float32)[None, :]
    table = math.sqrt(2.0 / BLOCK) * jnp.cos(math.pi * (2.0 * place + 1.0) * freq / (2.0 * BLOCK))
    return jnp.where(freq == 0.0, table * math.sqrt(0.5), table)


def analyze(matrix, basis_rows):
    row_count, col_count = matrix.shape
    blocks = matrix.reshape(row_count // BLOCK, BLOCK, col_count // BLOCK, BLOCK)
    halfway = jnp.einsum("kr,arbc->akbc", basis_rows, blocks, precision=lax.Precision.HIGHEST)
    result = jnp.einsum("akbc,lc->akbl", halfway, basis_rows, precision=lax.Precision.HIGHEST)
    return result.reshape(row_count // BLOCK, KEEP, col_count // BLOCK * KEEP)


def synthesize(coefficients, basis_rows):
    row_blocks, keep_rows, wide = coefficients.shape
    col_blocks = wide // KEEP
    shaped = coefficients.reshape(row_blocks, KEEP, col_blocks, KEEP)
    halfway = jnp.einsum("akbl,lc->akbc", shaped, basis_rows, precision=lax.Precision.HIGHEST)
    blocks = jnp.einsum("kr,akbc->arbc", basis_rows, halfway, precision=lax.Precision.HIGHEST)
    return blocks.reshape(row_blocks * BLOCK, col_blocks * BLOCK)


def token_product(inputs, grads):
    return lax.dot_general(
        inputs, grads, (((0,), (0,)), ((), ())), preferred_element_type=jnp.float32
    )


def body(activations, cotangent, momentum):
    rows_dev = momentum.shape[1]
    col_count = momentum.shape[2]
    groups = lax.axis_size("fsdp")
    features = lax.all_to_all(activations, "fsdp", split_axis=1, concat_axis=0, tiled=True)
    grads = lax.all_gather(cotangent, "fsdp", axis=0, tiled=True)
    gradient = token_product(features, grads)
    accum = 0.999 * momentum[0].astype(jnp.float32) + gradient
    basis_rows = dct_basis()
    local_coef = analyze(accum, basis_rows)
    summed = lax.psum(local_coef, "rep")
    mean_coefficients = summed / lax.axis_size("rep")
    recon = synthesize(mean_coefficients, basis_rows)
    squares = lax.psum(jnp.sum(recon * recon), "fsdp")
    scale_inv = lax.rsqrt(squares / (rows_dev * groups * col_count) + 1e-06)
    update = (recon * scale_inv).astype(jnp.bfloat16)
    new_momentum = (accum - recon).astype(jnp.bfloat16)[None]
    return (new_momentum, update)


def solution(mesh):
    placed = (P(("rep", "fsdp"), None), P(("rep", "fsdp"), None), P("rep", "fsdp", None))
    return jax.shard_map(
        body,
        mesh=mesh,
        in_specs=placed,
        out_specs=(P("rep", "fsdp", None), P("fsdp", None)),
        check_vma=False,
    )
```

profile of v0, /device:TPU:0, one launch (start us, length us, event | category | flops | bytes accessed | tf_op | source)
XLA Modules:
  0.0 233.5 jit_solution(5751827774081799893)
XLA Ops:
  7.2 4.1 %copy.12 = bf16[256,4096]{0,1:T(8,128)(2,1)} copy(bf16[256,4096]{1,0:T(8,128)(2,1)} %param.3) | data formatting | bytes 4194304 | tf_op args[0]
  11.2 0.0 copy-start.1
  11.2 4.4 %all-to-all-start = ((bf16[256,2,2048]{0,2,1:T(8,128)(2,1)}), bf16[256,2,2048]{0,2,1:T(8,128)(2,1)S(1)}, u32[]{:S(2)}, u32[]{:S(2)}) async-start(bf16[256,2,2048]{0,2,1:T(8,128)(2,1)} %bitcast.34), calls=%async_computation | async-start | bytes 4194304 | tf_op jit(solution)/shard_map/all_to_all | solution.py:46
  15.6 0.0 all-reduce.2.cloned.1.call-start
  15.6 0.0 copy-done.1
  15.6 31.4 %all_gather.3 = bf16[512,512]{1,0:T(8,128)(2,1)S(1)} all-gather(bf16[256,512]{1,0:T(8,128)(2,1)S(1)} %copy-done.1), channel_id=1, replica_groups=mesh['rep'=16,'fsdp'=2] {'fsdp'}, dimensions={0}, use_global_device_ids=true | all-gather | bytes 786432 | tf_op jit(solution)/shard_map/all_gather | solution.py:47
  47.1 0.0 all-to-all-done
  47.1 0.0 copy-start
  47.1 1.3 copy-done
  48.4 2.9 %copy.13 = bf16[2,256,2048]{2,1,0:T(8,128)(2,1)S(1)} copy(bf16[2,256,2048]{1,2,0:T(8,128)(2,1)} %bitcast.33) | data formatting | bytes 4194304 | tf_op jit(solution)/shard_map/all_to_all | solution.py:46
  51.3 4.8 %bitcast_add_fusion = f32[2048,512]{1,0:T(8,128)} fusion(bf16[1,2048,512]{2,1,0:T(8,128)(2,1)} %param.5, bf16[512,2048]{1,0:T(8,128)(2,1)S(1)} %bitcast.32, bf16[512,512]{1,0:T(8,128)(2,1)S(1)} %all_gather.3), kind=kOutput, calls=%fused_computation.3 | convolution fusion | flops 1076887552 | bytes 8912896 | tf_op jit(solution)/shard_map/dot_general | solution.py:37
  56.2 7.0 %reshape.36 = f32[32,64,8,64]{3,2,1,0:T(8,128)} reshape(f32[2048,512]{1,0:T(8,128)} %bitcast_add_fusion) | data formatting | bytes 8388608 | tf_op jit(solution)/shard_map/reshape | solution.py:21
  63.2 8.8 %fusion.5 = f32[32,16,8,64]{3,1,2,0:T(8,128)S(1)} fusion(f32[32,64,8,64]{3,2,1,0:T(8,128)} %reshape.36, f32[64]{0:T(128)S(1)} %add_multiply_fusion, pred[16]{0:T(512)(128)(4,1)S(1)} %iota_compare_fusion), kind=kOutput, calls=%fused_computation.10 | convolution fusion | flops 201331712 | bytes 5243152 | tf_op jit(solution)/shard_map/kr,arbc->akbc/dot_general | solution.py:22
  72.0 9.8 %fusion.3 = f32[32,16,8,16]{0,3,2,1:T(8,128)} fusion(f32[32,16,8,64]{3,1,2,0:T(8,128)S(1)} %fusion.5, f32[64]{0:T(128)S(1)} %add_multiply_fusion, pred[16]{0:T(512)(128)(4,1)S(1)} %iota_compare_fusion), kind=kOutput, calls=%fused_computation.8 | convolution fusion | flops 50336768 | bytes 1310992 | tf_op jit(solution)/shard_map/akbc,lc->akbl/dot_general | solution.py:23
  81.8 0.0 all-reduce.2.cloned.1.call-update
  81.9 93.7 %all-reduce.2.cloned.1.call-done = f32[32,16,128]{0,2,1:T(8,128)} async-done(((f32[32,16,128]{0,2,1:T(8,128)}), f32[32,16,128]{0,2,1:T(8,128)}) %all-reduce.2.cloned.1.call-update) | async-done | bytes 262160 | tf_op jit(solution)/shard_map/psum | solution.py:52
  175.6 1.3 broadcast_multiply_fusion
  176.9 1.8 copy.16
  178.7 1.9 fusion.9
  180.6 16.3 %multiply_reduce_fusion = (f32[]{:T(128)}, f32[32,64,8,64]{1,3,2,0:T(8,128)}) fusion(f32[32,16,8,64]{3,1,2,0:T(8,128)S(1)} %fusion.9, f32[64]{0:T(128)S(1)} %add_multiply_fusion, pred[16]{0:T(512)(128)(4,1)S(1)} %iota_compare_fusion), kind=kOutput, calls=%fused_computation.2 | convolution fusion | flops 203428864 | bytes 5243156 | tf_op jit(solution)/shard_map/kr,akbc->arbc/dot_general | solution.py:32
  196.9 5.5 %psum.15 = f32[]{:T(128)} all-reduce(f32[]{:T(128)} %get-tuple-element.4), channel_id=1, replica_groups=mesh['rep'=16,'fsdp'=2] {'fsdp'}, use_global_device_ids=true, to_apply=%region_2.3 | all-reduce | flops 1 | bytes 8 | tf_op jit(solution)/shard_map/psum | solution.py:55
  203.1 9.3 %copy.17 = f32[32,64,8,64]{3,2,1,0:T(8,128)} copy(f32[32,64,8,64]{1,3,2,0:T(8,128)} %get-tuple-element.5) | data formatting | bytes 8388608 | tf_op jit(solution)/shard_map/kr,akbc->arbc/transpose | solution.py:32
  212.4 7.5 %reshape.39 = f32[2048,512]{1,0:T(8,128)} reshape(f32[32,64,8,64]{3,2,1,0:T(8,128)} %copy.17) | data formatting | bytes 8388608 | tf_op jit(solution)/shard_map/reshape | solution.py:33
  219.9 6.7 %multiply_convert_fusion = (bf16[2048,512]{1,0:T(8,128)(2,1)}, bf16[1,2048,512]{2,1,0:T(8,128)(2,1)}) fusion(f32[2048,512]{1,0:T(8,128)} %reshape.39, f32[]{:T(128)S(6)} %rsqrt.3, f32[2048,512]{1,0:T(8,128)} %bitcast_add_fusion), kind=kLoop, calls=%fused_computation.4 | loop fusion | flops 4194304 | bytes 12582916 | tf_op jit(solution)/shard_map/convert_element_type | solution.py:57
  (2 shorter events, 0.0 us)
Async XLA Ops:
  11.2 4.4 %copy-start.1 = (bf16[256,512]{1,0:T(8,128)(2,1)S(1)}, bf16[256,512]{1,0:T(8,128)(2,1)}, u32[]{:S(2)}) copy-start(bf16[256,512]{1,0:T(8,128)(2,1)} %param.4) | copy-start | bytes 786436
  11.2 35.8 %all-to-all-start = ((bf16[256,2,2048]{0,2,1:T(8,128)(2,1)}), bf16[256,2,2048]{0,2,1:T(8,128)(2,1)S(1)}, u32[]{:S(2)}, u32[]{:S(2)}) async-start(bf16[256,2,2048]{0,2,1:T(8,128)(2,1)} %bitcast.34), calls=%async_computation | async-start | bytes 4194304 | tf_op jit(solution)/shard_map/all_to_all | solution.py:46
  15.6 160.0 %all-reduce.2.cloned.1.call-start = ((), (), s32[]{:S(2)}) async-start(), calls=%async_computation.1 | async-start | bytes 2097152 | tf_op jit(solution)/shard_map/psum | solution.py:52
  47.1 1.3 copy-start
Sparse Core Ops, SparseCore 0:
  82.0 93.5 all-reduce.1
where the time goes:
time: 234 us; the launch traced here: 233 us
  waiting for transfers between devices  93.8 us (40%)
  matrix products  41.6 us (18%)
  blocking collectives  37 us (16%)
  local copies, waits for them, and re-layouts  33.9 us (14%)
  between operations  14.8 us (6%)
  other arithmetic  8.05 us (3%)
  starting transfers between devices  4.37 us (2%)
    psum x1, waiting for transfers between devices, body(): summed = lax.psum(local_coef, 'rep')  93.7 us
    all_gather x1, blocking collectives, body(): grads = lax.all_gather(cotangent, 'fsdp', axis=0, tiled=True)  31.4 us
    dot_general x1, matrix products, synthesize(): jnp.einsum('kr,akbc->arbc', basis_rows, halfway, precision=lax.Precision....  16.3 us
    dot_general x1, matrix products, analyze(): jnp.einsum('akbc,lc->akbl', halfway, basis_rows, precision=lax.Precision....  9.85 us
    transpose x1, local copies, waits for them, and re-layouts, synthesize(): jnp.einsum('kr,akbc->arbc', basis_rows, halfway, precision=lax.Precision....  9.28 us
    dot_general x1, matrix products, analyze(): jnp.einsum('kr,arbc->akbc', basis_rows, blocks, precision=lax.Precision.H...  8.77 us
    reshape x1, local copies, waits for them, and re-layouts, synthesize(): return blocks.reshape(row_blocks * BLOCK, col_blocks * BLOCK)  7.48 us
    reshape x1, local copies, waits for them, and re-layouts, analyze(): matrix.reshape(row_count // BLOCK, BLOCK, col_count // BLOCK, BLOCK)  7.03 us
  transfers between devices with their start and end apart: 2, of which 1 were waited for; matrix products, arithmetic and copies ran while one was open for 0% of the time, Pallas kernels for 0%

commit v1 on v0

--- a/solution.py
+++ b/solution.py
@@ -1,12 +1,21 @@
+import functools
 import math
 
 import jax
 import jax.numpy as jnp
+import numpy as np
 from jax import lax
+from jax.experimental import pallas as pl
+from jax.experimental.pallas import tpu as pltpu
 from jax.sharding import PartitionSpec as P
 
 BLOCK = 64
 KEEP = 16
+CHUNK = 256
+FIRST = 4
+MESH = pl.DeviceIdType.MESH
+F32 = jnp.float32
+BF16 = jnp.bfloat16
 
 
 def dct_basis():
@@ -39,7 +48,7 @@
     )
 
 
-def body(activations, cotangent, momentum):
+def plain_body(activations, cotangent, momentum):
     rows_dev = momentum.shape[1]
     col_count = momentum.shape[2]
     groups = lax.axis_size("fsdp")
@@ -59,6 +68,300 @@
     return (new_momentum, update)
 
 
+def tables(cols):
+    freq = np.arange(KEEP, dtype=np.float64)[:, None]
+    place = np.arange(BLOCK, dtype=np.float64)[None, :]
+    basis = math.sqrt(2.0 / BLOCK) * np.cos(math.pi * (2.0 * place + 1.0) * freq / (2.0 * BLOCK))
+    basis[0] *= math.sqrt(0.5)
+    bf16 = np.dtype(jnp.bfloat16)
+
+    def split(full):
+        high = full.astype(bf16)
+        low = (full - high.astype(np.float64)).astype(bf16)
+        return high, low
+
+    col_high, col_low = split(np.kron(np.eye(cols // BLOCK), basis))
+    row_high, row_low = split(np.kron(np.eye(CHUNK // BLOCK), basis))
+    col_in = np.concatenate([col_high.T, col_low.T], 1)
+    row_in = np.concatenate([row_high, row_low], 0)
+    col_out = np.concatenate([col_high, col_high, col_low], 0)
+    row_out = np.concatenate([row_high.T, row_low.T, row_high.T, row_low.T], 1)
+    return col_in, row_in, col_out, row_out
+
+
+def halves(x):
+    high = x.astype(BF16)
+    low = (x - high.astype(F32)).astype(BF16)
+    return high, low
+
+
+def dot(a, b):
+    return jnp.dot(a, b, preferred_element_type=F32)
+
+
+def kernel(
+    act, cot, mom, col_in, row_in, col_out, row_out,
+    out_mom, out_upd,
+    a_own, a_oth, a_recv, c_own, c_recv, c_coef, m_own, accum, mid,
+    part, pair, parts, share, share_recv, gathered, upd, new,
+    load_sem, out_sem, bulk_send, bulk_recv, cot_sem, pair_sem,
+    rs_send, rs_recv, y_sem, ag_send, ag_recv, fw_send, fw_recv,
+    *, n_rep, n_chunks, n_elems,
+):
+    nq = n_rep // 2
+    rows = n_chunks * CHUNK
+    kept = n_chunks * (CHUNK // BLOCK * KEEP)
+    per_chunk = CHUNK // BLOCK * KEEP
+    half = kept // 2
+    piece = half // nq
+    wide = part.shape[2]
+    r = lax.axis_index("rep")
+    f = lax.axis_index("fsdp")
+    q = r // 2
+    c = r % 2
+    pal = 2 * q + (1 - c)
+    opp = 1 - f
+
+    def peer(d):
+        return 2 * lax.rem(q + d, nq) + c
+
+    barrier = pltpu.get_barrier_semaphore()
+    targets = [(r, opp), (pal, f)] + [(peer(d), f) for d in range(1, nq)]
+    for target in targets:
+        pl.semaphore_signal(barrier, inc=1, device_id=target, device_id_type=MESH)
+
+    own_cols = pl.ds(pl.multiple_of(f * rows, rows), rows)
+    oth_cols = pl.ds(pl.multiple_of(opp * rows, rows), rows)
+    loads = [
+        pltpu.make_async_copy(cot, c_own, load_sem.at[0]),
+        pltpu.make_async_copy(mom.at[0], m_own, load_sem.at[1]),
+        pltpu.make_async_copy(act.at[:, own_cols], a_own, load_sem.at[2]),
+        pltpu.make_async_copy(act.at[:, oth_cols], a_oth, load_sem.at[3]),
+    ]
+    for load in loads:
+        load.start()
+
+    def remote(src, dst, send, recv, target):
+        return pltpu.make_async_remote_copy(
+            src_ref=src, dst_ref=dst, send_sem=send, recv_sem=recv,
+            device_id=target, device_id_type=MESH,
+        )
+
+    cot_copy = remote(cot, c_recv, cot_sem.at[0], cot_sem.at[1], (r, opp))
+    bulk = []
+    for k in range(n_chunks):
+        cols = pl.ds(pl.multiple_of(opp * rows + k * CHUNK, CHUNK), CHUNK)
+        bulk.append(remote(act.at[:, cols], a_recv.at[k], bulk_send.at[k], bulk_recv.at[k], (r, opp)))
+
+    pl.semaphore_wait(barrier, len(targets))
+    cot_copy.start()
+    for k in range(min(FIRST, n_chunks)):
+        bulk[k].start()
+
+    loads[0].wait()
+    proj = dot(c_own[...], col_in[...])
+    high, low = halves(proj[:, :wide] + proj[:, wide:])
+    c_coef[:, :wide] = high
+    c_coef[:, wide:] = low
+
+    def chunk_coefs(slot, h, g):
+        hh, hl = halves(h)
+        y = dot(row_in[...], jnp.concatenate([hh, hl], axis=1))
+        y = y[:, :wide] + y[:, wide:]
+        part[slot, pl.ds(pl.multiple_of(g * per_chunk, per_chunk), per_chunk), :] = y[:per_chunk] + y[per_chunk:]
+
+    loads[1].wait()
+    loads[2].wait()
+
+    def own_step(g, carry):
+        span = pl.ds(pl.multiple_of(g * CHUNK, CHUNK), CHUNK)
+        h = token_product(a_own[:, span], c_coef[...])
+        m = dot(m_own[span, :], col_in[...])
+        h = h[:, :wide] + h[:, wide:] + 0.999 * (m[:, :wide] + m[:, wide:])
+        chunk_coefs(0, h, g)
+        return carry
+
+    lax.fori_loop(0, n_chunks, own_step, 0)
+    loads[3].wait()
+
+    def oth_step(g, carry):
+        span = pl.ds(pl.multiple_of(g * CHUNK, CHUNK), CHUNK)
+        h = token_product(a_oth[:, span], c_coef[...])
+        chunk_coefs(1, h[:, :wide] + h[:, wide:], g)
+        return carry
+
+    lax.fori_loop(0, n_chunks, oth_step, 0)
+
+    pal_rows = pl.ds(pl.multiple_of((1 - c) * half, half), half)
+    pair_copy = remote(part.at[:, pal_rows], pair, pair_sem.at[0], pair_sem.at[1], (pal, f))
+    pair_copy.start()
+
+    def grad_step(g, carry):
+        span = pl.ds(pl.multiple_of(g * CHUNK, CHUNK), CHUNK)
+        accum[span, :] = 0.999 * m_own[span, :].astype(F32) + token_product(a_own[:, span], c_own[...])
+        return carry
+
+    lax.fori_loop(0, n_chunks // 2, grad_step, 0)
+
+    pair_copy.wait()
+    my_rows = pl.ds(pl.multiple_of(c * half, half), half)
+    pair[...] = pair[...] + part[:, my_rows, :]
+
+    scatter = []
+    for d in range(1, nq):
+        at = pl.ds(pl.multiple_of(lax.rem(q + d, nq) * piece, piece), piece)
+        copy = remote(pair.at[:, at], parts.at[d], rs_send.at[d], rs_recv.at[d], (peer(d), f))
+        copy.start()
+        scatter.append(copy)
+
+    lax.fori_loop(n_chunks // 2, n_chunks, grad_step, 0)
+
+    total = pair[:, pl.ds(pl.multiple_of(q * piece, piece), piece), :]
+    for d in range(1, nq):
+        scatter[d - 1].wait()
+        total = total + parts[d]
+    share[...] = total
+
+    y_copy = remote(share, share_recv, y_sem.at[0], y_sem.at[1], (r, opp))
+    y_copy.start()
+    for k in range(min(FIRST, n_chunks), n_chunks):
+        bulk[k].start()
+    y_copy.wait()
+    mine = (share[0] + share_recv[1]) / n_rep
+    other = (share[1] + share_recv[0]) / n_rep
+    squares = (mine * mine + other * other).reshape(piece // 8, 8, wide)
+    gathered[c, q, :piece] = mine
+    gathered[c, q, piece:] = jnp.sum(squares, axis=0)
+
+    spread = []
+    for d in range(1, nq):
+        copy = remote(gathered.at[c, q], gathered.at[c, q], ag_send.at[d], ag_recv.at[d], (peer(d), f))
+        copy.start()
+        spread.append(copy)
+    forward = []
+    for d in range(nq):
+        src = lax.rem(q - d + nq, nq)
+        if d > 0:
+            spread[d - 1].wait_recv()
+        copy = remote(gathered.at[c, src], gathered.at[c, src], fw_send.at[d], fw_recv.at[d], (pal, f))
+        copy.start()
+        forward.append(copy)
+    for d in range(nq):
+        forward[d].wait()
+        if d > 0:
+            spread[d - 1].wait_send()
+
+    everything = gathered[...]
+    coefs = everything[:, :, :piece].reshape(kept, wide)
+    sq = everything[:, :, piece:].reshape(n_rep * 8, wide)
+    sq = jnp.sum(jnp.sum(sq, axis=0, keepdims=True), axis=1, keepdims=True)
+    scale = lax.rsqrt(sq / n_elems + 1e-06)
+    ch, cl = halves(coefs)
+    mid[...] = dot(jnp.concatenate([ch, cl, ch], axis=1), col_out[...])
+
+    def recon_step(g, carry):
+        span = pl.ds(pl.multiple_of(g * CHUNK, CHUNK), CHUNK)
+        x = mid[pl.ds(pl.multiple_of(g * per_chunk, per_chunk), per_chunk), :]
+        xh, xl = halves(x)
+        recon = dot(row_out[...], jnp.concatenate([xh, xh, xl, xl], axis=0))
+        upd[span, :] = (recon * scale).astype(BF16)
+        accum[span, :] = accum[span, :] - recon
+        return carry
+
+    lax.fori_loop(0, n_chunks, recon_step, 0)
+    upd_out = pltpu.make_async_copy(upd, out_upd, out_sem.at[0])
+    upd_out.start()
+
+    cot_copy.wait()
+    outs = []
+    for k in range(n_chunks):
+        bulk[k].wait()
+        span = slice(k * CHUNK, (k + 1) * CHUNK)
+        new[span, :] = (accum[span, :] + token_product(a_recv[k], c_recv[...])).astype(BF16)
+        copy = pltpu.make_async_copy(new.at[span], out_mom.at[0, span], out_sem.at[k + 1])
+        copy.start()
+        outs.append(copy)
+    upd_out.wait()
+    for copy in outs:
+        copy.wait()
+
+
+def kernel_body(activations, cotangent, momentum):
+    tokens = activations.shape[0]
+    rows, cols = momentum.shape[1], momentum.shape[2]
+    n_rep = lax.axis_size("rep")
+    groups = lax.axis_size("fsdp")
+    n_chunks = rows // CHUNK
+    wide = cols // BLOCK * KEEP
+    kept = rows // BLOCK * KEEP
+    nq = n_rep // 2
+    half = kept // 2
+    piece = half // nq
+    any_spec = pl.BlockSpec(memory_space=pl.ANY)
+    vmem_spec = pl.BlockSpec(memory_space=pltpu.VMEM)
+    dma = pltpu.SemaphoreType.DMA
+    return pl.pallas_call(
+        functools.partial(kernel, n_rep=n_rep, n_chunks=n_chunks, n_elems=rows * groups * cols),
+        out_shape=(
+            jax.ShapeDtypeStruct((1, rows, cols), BF16),
+            jax.ShapeDtypeStruct((rows, cols), BF16),
+        ),
+        in_specs=[any_spec] * 3 + [vmem_spec] * 4,
+        out_specs=(any_spec, any_spec),
+        scratch_shapes=[
+            pltpu.VMEM((tokens, rows), BF16),
+            pltpu.VMEM((tokens, rows), BF16),
+            pltpu.VMEM((n_chunks, tokens, CHUNK), BF16),
+            pltpu.VMEM((tokens, cols), BF16),
+            pltpu.VMEM((tokens, cols), BF16),
+            pltpu.VMEM((tokens, 2 * wide), BF16),
+            pltpu.VMEM((rows, cols), BF16),
+            pltpu.VMEM((rows, cols), F32),
+            pltpu.VMEM((kept, cols), F32),
+            pltpu.VMEM((2, kept, wide), F32),
+            pltpu.VMEM((2, half, wide), F32),
+            pltpu.VMEM((nq, 2, piece, wide), F32),
+            pltpu.VMEM((2, piece, wide), F32),
+            pltpu.VMEM((2, piece, wide), F32),
+            pltpu.VMEM((2, nq, piece + 8, wide), F32),
+            pltpu.VMEM((rows, cols), BF16),
+            pltpu.VMEM((rows, cols), BF16),
+            dma((4,)),
+            dma((n_chunks + 1,)),
+            dma((n_chunks,)),
+            dma((n_chunks,)),
+            dma((2,)),
+            dma((2,)),
+            dma((nq,)),
+            dma((nq,)),
+            dma((2,)),
+            dma((nq,)),
+            dma((nq,)),
+            dma((nq,)),
+            dma((nq,)),
+        ],
+        compiler_params=pltpu.CompilerParams(
+            collective_id=0, has_side_effects=True, vmem_limit_bytes=48 * 2**20
+        ),
+    )(activations, cotangent, momentum, *(jnp.asarray(t) for t in tables(cols)))
+
+
+def body(activations, cotangent, momentum):
+    n_rep = lax.axis_size("rep")
+    rows, cols = momentum.shape[1], momentum.shape[2]
+    wide = cols // BLOCK * KEEP
+    kept = rows // BLOCK * KEEP
+    fits = (
+        lax.axis_size("fsdp") == 2
+        and n_rep % 2 == 0
+        and kept % (8 * n_rep) == 0
+        and rows % CHUNK == 0
+        and wide % 128 == 0
+        and activations.shape[0] % 128 == 0
+    )
+    return (kernel_body if fits else plain_body)(activations, cotangent, momentum)
+
+
 def solution(mesh):
     placed = (P(("rep", "fsdp"), None), P(("rep", "fsdp"), None), P("rep", "fsdp", None))
     return jax.shard_map(

time: 234 us -> 45.9 us (0.20)
  waiting for transfers between devices: 93.8 us -> 0 us
  matrix products: 41.6 us -> 0 us
  Pallas kernels: 0 us -> 37.7 us
  blocking collectives: 37 us -> 0 us
  local copies, waits for them, and re-layouts: 33.9 us -> 7.27 us
  between operations: 14.8 us -> 0.65 us
  other arithmetic: 8.05 us -> 0 us
  starting transfers between devices: 4.37 us -> 0 us
    psum x1 -> x0, waiting for transfers between devices: 93.7 us -> none  [body(): summed = lax.psum(local_coef, 'rep')]
    dot_general x5 -> x0, matrix products: 41.6 us -> none  [the longest x1 16.3 us: synthesize(): jnp.einsum('kr,akbc->arbc', basis_rows, halfway, precision=lax.Precision....]
    pallas_call x0 -> x1, Pallas kernels: none -> 37.7 us  [kernel_body(): pl.pallas_call(functools.partial(kernel, n_rep=n_rep, n_chunks=n_chunks,...]
    all_gather x1 -> x0, blocking collectives: 31.4 us -> none  [body(): grads = lax.all_gather(cotangent, 'fsdp', axis=0, tiled=True)]
    reshape x3 -> x0, local copies, waits for them, and re-layouts: 16.3 us -> none  [the longest x1 7.48 us: synthesize(): return blocks.reshape(row_blocks * BLOCK, col_blocks * BLOCK)]
    transpose x1 -> x0, local copies, waits for them, and re-layouts: 9.28 us -> none  [synthesize(): jnp.einsum('kr,akbc->arbc', basis_rows, halfway, precision=lax.Precision....]
    convert_element_type x1 -> x0, other arithmetic: 6.72 us -> none  [body(): update = (recon * scale_inv).astype(jnp.bfloat16)]
    psum x1 -> x0, blocking collectives: 5.55 us -> none  [body(): squares = lax.psum(jnp.sum(recon * recon), 'fsdp')]
  transfers between devices with their start and end apart: 2 -> 0, of which waited for: 1 -> 0; matrix products, arithmetic and copies ran while one was open for 0% -> 0% of each run, Pallas kernels for 0% -> 0%
where the time goes in v1:
time: 45.9 us; the launch traced here: 45.6 us
  Pallas kernels  37.7 us (82%)
  local copies, waits for them, and re-layouts  7.27 us (16%)
  between operations  0.65 us (1%)
    pallas_call x1, Pallas kernels, kernel_body(): pl.pallas_call(functools.partial(kernel, n_rep=n_rep, n_chunks=n_chunks,...  37.7 us
    unnamed x12, local copies, waits for them, and re-layouts  7.27 us

profile of v1, /device:TPU:0, one launch (start us, length us, event | category | flops | bytes accessed | tf_op | source)
XLA Modules:
  0.0 45.6 jit_solution(16430780406138247050)
XLA Ops:
  0.6 0.0 copy-start
  0.6 1.0 %copy-done = bf16[384,512]{1,0:T(8,128)(2,1)S(1)} copy-done((bf16[384,512]{1,0:T(8,128)(2,1)S(1)}, bf16[384,512]{1,0:T(8,128)(2,1)}, u32[]{:S(2)}) %copy-start) | copy-done | bytes 393240
  1.6 0.0 copy-start.1
  1.6 0.9 %copy-done.1 = bf16[256,512]{1,0:T(8,128)(2,1)S(1)} copy-done((bf16[256,512]{1,0:T(8,128)(2,1)S(1)}, bf16[256,512]{1,0:T(8,128)(2,1)}, u32[]{:S(2)}) %copy-start.1) | copy-done | bytes 262168
  2.6 0.0 copy-start.2
  2.6 0.9 %copy-done.2 = bf16[512,256]{1,0:T(8,128)(2,1)S(1)} copy-done((bf16[512,256]{1,0:T(8,128)(2,1)S(1)}, bf16[512,256]{1,0:T(8,128)(2,1)}, u32[]{:S(2)}) %copy-start.2) | copy-done | bytes 262168
  3.5 0.0 copy-start.3
  3.5 0.9 %copy-done.3 = bf16[256,256]{1,0:T(8,128)(2,1)S(1)} copy-done((bf16[256,256]{1,0:T(8,128)(2,1)S(1)}, bf16[256,256]{1,0:T(8,128)(2,1)}, u32[]{:S(2)}) %copy-start.3) | copy-done | bytes 131096
  4.4 0.0 copy-start.4
  4.4 0.8 %copy-done.4 = bf16[128,256]{1,0:T(8,128)(2,1)S(1)} copy-done((bf16[128,256]{1,0:T(8,128)(2,1)S(1)}, bf16[128,256]{1,0:T(8,128)(2,1)}, u32[]{:S(2)}) %copy-start.4) | copy-done | bytes 65560
  5.3 37.7 %shard_map.86 = (bf16[1,2048,512]{2,1,0:T(8,128)(2,1)S(1)}, bf16[2048,512]{1,0:T(8,128)(2,1)S(1)}) custom-call(bf16[256,4096]{1,0:T(8,128)(2,1)} %act.1, bf16[256,512]{1,0:T(8,128)(2,1)S(1)} %copy-done.1, bf16[1,2048,512]{2,1,0:T(8,128)(2,1)} %mom.1, bf16[512,256]{1,0:T(8,128)(2,1)S(1)} %copy-done.2, bf16[128,256]{1,0:T(8,128)(2,1)S(1)} %copy-done.4, ...), custom_call_target="tpu_custom_call" | custom-call | tf_op jit(solution)/shard_map/pallas_call | solution.py:303
  43.0 1.3 %copy.11 = bf16[1,2048,512]{2,1,0:T(8,128)(2,1)} copy(bf16[1,2048,512]{2,1,0:T(8,128)(2,1)S(1)} %get-tuple-element.4) | data formatting | bytes 4194304
  44.3 1.3 %copy.12 = bf16[2048,512]{1,0:T(8,128)(2,1)} copy(bf16[2048,512]{1,0:T(8,128)(2,1)S(1)} %get-tuple-element.5) | data formatting | bytes 4194304
Async XLA Ops:
  0.6 1.0 %copy-start = (bf16[384,512]{1,0:T(8,128)(2,1)S(1)}, bf16[384,512]{1,0:T(8,128)(2,1)}, u32[]{:S(2)}) copy-start(bf16[384,512]{1,0:T(8,128)(2,1)} %constant.10.clone.col_out) | copy-start | bytes 1179652
  1.6 0.9 %copy-start.1 = (bf16[256,512]{1,0:T(8,128)(2,1)S(1)}, bf16[256,512]{1,0:T(8,128)(2,1)}, u32[]{:S(2)}) copy-start(bf16[256,512]{1,0:T(8,128)(2,1)} %cot.1) | copy-start | bytes 786436
  2.6 0.9 %copy-start.2 = (bf16[512,256]{1,0:T(8,128)(2,1)S(1)}, bf16[512,256]{1,0:T(8,128)(2,1)}, u32[]{:S(2)}) copy-start(bf16[512,256]{1,0:T(8,128)(2,1)} %constant.8.clone.col_in) | copy-start | bytes 786436
  3.5 0.9 %copy-start.3 = (bf16[256,256]{1,0:T(8,128)(2,1)S(1)}, bf16[256,256]{1,0:T(8,128)(2,1)}, u32[]{:S(2)}) copy-start(bf16[256,256]{1,0:T(8,128)(2,1)} %constant.11.clone.row_out) | copy-start | bytes 393220
  4.4 0.8 %copy-start.4 = (bf16[128,256]{1,0:T(8,128)(2,1)S(1)}, bf16[128,256]{1,0:T(8,128)(2,1)}, u32[]{:S(2)}) copy-start(bf16[128,256]{1,0:T(8,128)(2,1)} %constant.9.clone.row_in) | copy-start | bytes 196612

commit v2 on v1

--- a/solution.py
+++ b/solution.py
@@ -3,7 +3,6 @@
 
 import jax
 import jax.numpy as jnp
-import numpy as np
 from jax import lax
 from jax.experimental import pallas as pl
 from jax.experimental.pallas import tpu as pltpu
@@ -68,25 +67,15 @@
     return (new_momentum, update)
 
 
-def tables(cols):
-    freq = np.arange(KEEP, dtype=np.float64)[:, None]
-    place = np.arange(BLOCK, dtype=np.float64)[None, :]
-    basis = math.sqrt(2.0 / BLOCK) * np.cos(math.pi * (2.0 * place + 1.0) * freq / (2.0 * BLOCK))
-    basis[0] *= math.sqrt(0.5)
-    bf16 = np.dtype(jnp.bfloat16)
-
-    def split(full):
-        high = full.astype(bf16)
-        low = (full - high.astype(np.float64)).astype(bf16)
-        return high, low
-
-    col_high, col_low = split(np.kron(np.eye(cols // BLOCK), basis))
-    row_high, row_low = split(np.kron(np.eye(CHUNK // BLOCK), basis))
-    col_in = np.concatenate([col_high.T, col_low.T], 1)
-    row_in = np.concatenate([row_high, row_low], 0)
-    col_out = np.concatenate([col_high, col_high, col_low], 0)
-    row_out = np.concatenate([row_high.T, row_low.T, row_high.T, row_low.T], 1)
-    return col_in, row_in, col_out, row_out
+def block_basis(kept, full):
+    k = lax.broadcasted_iota(jnp.int32, (kept, full), 0)
+    n = lax.broadcasted_iota(jnp.int32, (kept, full), 1)
+    freq = k & (KEEP - 1)
+    turn = ((2 * (n & (BLOCK - 1)) + 1) * freq) & (4 * BLOCK - 1)
+    table = math.sqrt(2.0 / BLOCK) * jnp.cos(turn.astype(F32) * (math.pi / (2.0 * BLOCK)))
+    table = jnp.where(freq == 0, math.sqrt(1.0 / BLOCK), table)
+    inside = (k >> int(math.log2(KEEP))) == (n >> int(math.log2(BLOCK)))
+    return halves(jnp.where(inside, table, 0.0))
 
 
 def halves(x):
@@ -99,12 +88,17 @@
     return jnp.dot(a, b, preferred_element_type=F32)
 
 
+def dot_rows(a, b):
+    return lax.dot_general(a, b, (((1,), (1,)), ((), ())), preferred_element_type=F32)
+
+
 def kernel(
-    act, cot, mom, col_in, row_in, col_out, row_out,
-    out_mom, out_upd,
+    act, cot, mom,
+    new, upd,
     a_own, a_oth, a_recv, c_own, c_recv, c_coef, m_own, accum, mid,
-    part, pair, parts, share, share_recv, gathered, upd, new,
-    load_sem, out_sem, bulk_send, bulk_recv, cot_sem, pair_sem,
+    part, pair, parts, share, share_recv, gathered,
+    col_basis, row_in, row_out,
+    load_sem, bulk_send, bulk_recv, cot_sem, pair_sem,
     rs_send, rs_recv, y_sem, ag_send, ag_recv, fw_send, fw_recv,
     *, n_rep, n_chunks, n_elems,
 ):
@@ -138,8 +132,8 @@
         pltpu.make_async_copy(act.at[:, own_cols], a_own, load_sem.at[2]),
         pltpu.make_async_copy(act.at[:, oth_cols], a_oth, load_sem.at[3]),
     ]
-    for load in loads:
-        load.start()
+    for at in (0, 2, 1, 3):
+        loads[at].start()
 
     def remote(src, dst, send, recv, target):
         return pltpu.make_async_remote_copy(
@@ -153,13 +147,22 @@
         cols = pl.ds(pl.multiple_of(opp * rows + k * CHUNK, CHUNK), CHUNK)
         bulk.append(remote(act.at[:, cols], a_recv.at[k], bulk_send.at[k], bulk_recv.at[k], (r, opp)))
 
+    col_high, col_low = block_basis(wide, col_basis.shape[1])
+    col_basis[:wide] = col_high
+    col_basis[wide : 2 * wide] = col_high
+    col_basis[2 * wide :] = col_low
+    row_high, row_low = block_basis(per_chunk, CHUNK)
+    row_in[:per_chunk] = row_high
+    row_in[per_chunk:] = row_low
+    row_out[...] = jnp.concatenate([row_high, row_low, row_high, row_low], axis=0).T
+
     pl.semaphore_wait(barrier, len(targets))
     cot_copy.start()
     for k in range(min(FIRST, n_chunks)):
         bulk[k].start()
 
     loads[0].wait()
-    proj = dot(c_own[...], col_in[...])
+    proj = dot_rows(c_own[...], col_basis[wide:])
     high, low = halves(proj[:, :wide] + proj[:, wide:])
     c_coef[:, :wide] = high
     c_coef[:, wide:] = low
@@ -176,7 +179,7 @@
     def own_step(g, carry):
         span = pl.ds(pl.multiple_of(g * CHUNK, CHUNK), CHUNK)
         h = token_product(a_own[:, span], c_coef[...])
-        m = dot(m_own[span, :], col_in[...])
+        m = dot_rows(m_own[span, :], col_basis[wide:])
         h = h[:, :wide] + h[:, wide:] + 0.999 * (m[:, :wide] + m[:, wide:])
         chunk_coefs(0, h, g)
         return carry
@@ -257,7 +260,7 @@
     sq = jnp.sum(jnp.sum(sq, axis=0, keepdims=True), axis=1, keepdims=True)
     scale = lax.rsqrt(sq / n_elems + 1e-06)
     ch, cl = halves(coefs)
-    mid[...] = dot(jnp.concatenate([ch, cl, ch], axis=1), col_out[...])
+    mid[...] = dot(jnp.concatenate([ch, cl, ch], axis=1), col_basis[...])
 
     def recon_step(g, carry):
         span = pl.ds(pl.multiple_of(g * CHUNK, CHUNK), CHUNK)
@@ -269,21 +272,11 @@
         return carry
 
     lax.fori_loop(0, n_chunks, recon_step, 0)
-    upd_out = pltpu.make_async_copy(upd, out_upd, out_sem.at[0])
-    upd_out.start()
-
     cot_copy.wait()
-    outs = []
     for k in range(n_chunks):
         bulk[k].wait()
         span = slice(k * CHUNK, (k + 1) * CHUNK)
-        new[span, :] = (accum[span, :] + token_product(a_recv[k], c_recv[...])).astype(BF16)
-        copy = pltpu.make_async_copy(new.at[span], out_mom.at[0, span], out_sem.at[k + 1])
-        copy.start()
-        outs.append(copy)
-    upd_out.wait()
-    for copy in outs:
-        copy.wait()
+        new[0, span, :] = (accum[span, :] + token_product(a_recv[k], c_recv[...])).astype(BF16)
 
 
 def kernel_body(activations, cotangent, momentum):
@@ -294,10 +287,11 @@
     n_chunks = rows // CHUNK
     wide = cols // BLOCK * KEEP
     kept = rows // BLOCK * KEEP
+    per_chunk = CHUNK // BLOCK * KEEP
     nq = n_rep // 2
     half = kept // 2
     piece = half // nq
-    any_spec = pl.BlockSpec(memory_space=pl.ANY)
+    hbm_spec = pl.BlockSpec(memory_space=pltpu.HBM)
     vmem_spec = pl.BlockSpec(memory_space=pltpu.VMEM)
     dma = pltpu.SemaphoreType.DMA
     return pl.pallas_call(
@@ -306,8 +300,8 @@
             jax.ShapeDtypeStruct((1, rows, cols), BF16),
             jax.ShapeDtypeStruct((rows, cols), BF16),
         ),
-        in_specs=[any_spec] * 3 + [vmem_spec] * 4,
-        out_specs=(any_spec, any_spec),
+        in_specs=[hbm_spec] * 3,
+        out_specs=(vmem_spec, vmem_spec),
         scratch_shapes=[
             pltpu.VMEM((tokens, rows), BF16),
             pltpu.VMEM((tokens, rows), BF16),
@@ -324,10 +318,10 @@
             pltpu.VMEM((2, piece, wide), F32),
             pltpu.VMEM((2, piece, wide), F32),
             pltpu.VMEM((2, nq, piece + 8, wide), F32),
-            pltpu.VMEM((rows, cols), BF16),
-            pltpu.VMEM((rows, cols), BF16),
+            pltpu.VMEM((3 * wide, cols), BF16),
+            pltpu.VMEM((2 * per_chunk, CHUNK), BF16),
+            pltpu.VMEM((CHUNK, 4 * per_chunk), BF16),
             dma((4,)),
-            dma((n_chunks + 1,)),
             dma((n_chunks,)),
             dma((n_chunks,)),
             dma((2,)),
@@ -343,7 +337,7 @@
         compiler_params=pltpu.CompilerParams(
             collective_id=0, has_side_effects=True, vmem_limit_bytes=48 * 2**20
         ),
-    )(activations, cotangent, momentum, *(jnp.asarray(t) for t in tables(cols)))
+    )(activations, cotangent, momentum)
 
 
 def body(activations, cotangent, momentum):

time: 45.9 us -> 42 us (0.915)
  local copies, waits for them, and re-layouts: 7.27 us -> 3.58 us
    unnamed x12 -> x4, local copies, waits for them, and re-layouts: 7.27 us -> 3.58 us
where the time goes in v2:
time: 42 us; the launch traced here: 41.8 us
  Pallas kernels  37.6 us (90%)
  local copies, waits for them, and re-layouts  3.58 us (9%)
  between operations  0.65 us (2%)
    pallas_call x1, Pallas kernels, kernel_body(): pl.pallas_call(functools.partial(kernel, n_rep=n_rep, n_chunks=n_chunks,...  37.6 us
    unnamed x4, local copies, waits for them, and re-layouts  3.58 us

profile of v2, /device:TPU:0, one launch (start us, length us, event | category | flops | bytes accessed | tf_op | source)
XLA Modules:
  0.0 41.8 jit_solution(10049074193320531110)
XLA Ops:
  0.6 0.0 copy-start
  0.6 0.9 %copy-done = bf16[256,512]{1,0:T(8,128)(2,1)S(1)} copy-done((bf16[256,512]{1,0:T(8,128)(2,1)S(1)}, bf16[256,512]{1,0:T(8,128)(2,1)}, u32[]{:S(2)}) %copy-start) | copy-done | bytes 262168
  1.6 37.6 %shard_map.50 = (bf16[1,2048,512]{2,1,0:T(8,128)(2,1)S(1)}, bf16[2048,512]{1,0:T(8,128)(2,1)S(1)}) custom-call(bf16[256,4096]{1,0:T(8,128)(2,1)} %act.1, bf16[256,512]{1,0:T(8,128)(2,1)S(1)} %copy-done, bf16[1,2048,512]{2,1,0:T(8,128)(2,1)} %mom.1), custom_call_target="tpu_custom_call" | custom-call | tf_op jit(solution)/shard_map/pallas_call | solution.py:297
  39.2 1.3 %copy.7 = bf16[1,2048,512]{2,1,0:T(8,128)(2,1)} copy(bf16[1,2048,512]{2,1,0:T(8,128)(2,1)S(1)} %get-tuple-element.4) | data formatting | bytes 4194304
  40.5 1.3 %copy.8 = bf16[2048,512]{1,0:T(8,128)(2,1)} copy(bf16[2048,512]{1,0:T(8,128)(2,1)S(1)} %get-tuple-element.5) | data formatting | bytes 4194304
Async XLA Ops:
  0.6 1.0 %copy-start = (bf16[256,512]{1,0:T(8,128)(2,1)S(1)}, bf16[256,512]{1,0:T(8,128)(2,1)}, u32[]{:S(2)}) copy-start(bf16[256,512]{1,0:T(8,128)(2,1)} %cot.1) | copy-start | bytes 786436
